TPU v7x, 32 devices: a whole 2x2x4 slice. The times are simulated.
32 devices in a mesh: crops: 2 (over x), rows: 16 (over z, y, core).
Axes of the slice: x: 2, y: 2, z: 4, core: 2. Of those that a mesh axis runs over, the one named last changes fastest.
Arguments:
- features: bfloat16 [64, 128, 2048], P(('crops', 'rows')), parts along dimension 0, may hold values from -6 to 6
- bn_scale: float32 [2048], replicated, may hold values from 0.25 to 1.75
- bn_shift: float32 [2048], replicated, may hold values from -0.6 to 0.6
- atrous_weight: bfloat16 [3, 3, 2048, 256], replicated, may hold values from -0.046875 to 0.046875
- cotangent: bfloat16 [64, 128, 256], P(('crops', 'rows')), parts along dimension 0, may hold values from -0.59765625 to 0.59765625
Outputs:
- branch_out: bfloat16 [64, 128, 256], P(('crops', 'rows')), parts along dimension 0
- feature_grad: bfloat16 [64, 128, 2048], P(('crops', 'rows')), parts along dimension 0
- weight_grad: float32 [6, 3, 2048, 256], P('crops', None, 'rows'), parts along dimension 0
There are 2 independent parts, one for each index of `crops`. A program takes and returns all parts, laid end to end along the dimension named above; an argument that names none is the same for every part. Nothing has to cross between parts.
All inputs are finite; a program needn't handle non-finite values.
Results may differ from a plain program's by a relative error of at most 0.0051.
Values may be sent and summed in bfloat16 or wider, within the bound.
A program may use at most 128 MiB of HBM per device.

v0:
```python
import jax
import jax.numpy as jnp
from jax import lax
from jax.sharding import PartitionSpec as P

RATE = 12


def from_behind(array, axis, by):
    devices = lax.axis_size(axis)
    pairs = [(i, i + by) for i in range(devices) if 0 <= i + by < devices]
    return lax.ppermute(array, axis, pairs)


def branch_forward(blocks, atrous_weight, width):
    total = jnp.zeros(blocks[1].shape[:2] + (atrous_weight.shape[3],), jnp.float32)
    for row_tap in range(3):
        padded = jnp.pad(blocks[row_tap], ((0, 0), (RATE, RATE), (0, 0)))
        for col_tap in range(3):
            window = padded[:, RATE * col_tap : RATE * col_tap + width]
            total = total + jnp.einsum(
                "hwc,ck->hwk",
                window,
                atrous_weight[row_tap, col_tap],
                preferred_element_type=jnp.float32,
            )
    return total


def spatial_act_grad(blocks, atrous_weight, width):
    total = jnp.zeros(blocks[1].shape[:2] + (atrous_weight.shape[2],), jnp.float32)
    for row_tap in range(3):
        padded = jnp.pad(blocks[row_tap], ((0, 0), (RATE, RATE), (0, 0)))
        for col_tap in range(3):
            window = padded[:, RATE * (2 - col_tap) : RATE * (2 - col_tap) + width]
            total = total + jnp.einsum(
                "hwk,ck->hwc",
                window,
                atrous_weight[row_tap, col_tap],
                preferred_element_type=jnp.float32,
            )
    return total


def spatial_kernel_terms(blocks, cotangent, width):
    kernel_rows = []
    for row_tap in range(3):
        padded = jnp.pad(blocks[row_tap], ((0, 0), (RATE, RATE), (0, 0)))
        kernel_cols = []
        for col_tap in range(3):
            window = padded[:, RATE * col_tap : RATE * col_tap + width]
            kernel_cols.append(
                jnp.einsum("hwc,hwk->ck", window, cotangent, preferred_element_type=jnp.float32)
            )
        kernel_rows.append(jnp.stack(kernel_cols))
    return jnp.stack(kernel_rows)


def per_device(features, bn_scale, bn_shift, atrous_weight, cotangent):
    local_rows, width, chans = features.shape
    distance = RATE // local_rows
    pre_act = features.astype(jnp.float32) * bn_scale + bn_shift
    activated = jnp.maximum(pre_act, 0.0).astype(jnp.bfloat16)
    act_above, cot_above = from_behind((activated, cotangent), "rows", distance)
    act_below, cot_below = from_behind((activated, cotangent), "rows", -distance)
    blocks = (act_above, activated, act_below)
    branch = branch_forward(blocks, atrous_weight, width)
    act_grad = spatial_act_grad((cot_below, cotangent, cot_above), atrous_weight, width)
    terms = spatial_kernel_terms(blocks, cotangent, width)
    weight_grad = lax.psum_scatter(terms, "rows", scatter_dimension=2, tiled=True)
    branch_out = branch.astype(jnp.bfloat16)
    rounded = lax.optimization_barrier(act_grad.astype(jnp.bfloat16)).astype(jnp.float32)
    feature_grad = (bn_scale * jnp.where(pre_act > 0, rounded, 0.0)).astype(jnp.bfloat16)
    return (branch_out, feature_grad, weight_grad)


def solution(mesh):
    return jax.shard_map(
        per_device,
        mesh=mesh,
        in_specs=(
            P(("crops", "rows"), None, None),
            P(),
            P(),
            P(),
            P(("crops", "rows"), None, None),
        ),
        out_specs=(
            P(("crops", "rows"), None, None),
            P(("crops", "rows"), None, None),
            P("crops", None, "rows", None),
        ),
        check_vma=False,
    )
```

profile of v0, /device:TPU:5, one launch (start us, length us, event | category | flops | bytes accessed | tf_op | source)
XLA Modules:
  0.0 295.4 jit_solution(16855704651853069021)
XLA Ops:
  7.2 0.0 reduce-scatter.2.cloned.1.call-start
  7.2 4.2 %collective-permute-start.3 = (bf16[2,128,256]{2,1,0:T(8,128)(2,1)}, bf16[2,128,256]{2,1,0:T(8,128)(2,1)S(1)}, u32[]{:S(2)}, u32[]{:S(2)}) collective-permute-start(bf16[2,128,256]{2,1,0:T(8,128)(2,1)} %param.9), channel_id=1, source_target_pairs={{0,6},{1,7},{2,8},{3,9},{4,10},{5,11},{6,12},{7,13},{8,14},{9,15},... | collective-permute-start | bytes 393224 | tf_op jit(solution)/shard_map/ppermute | solution.py:12
  11.4 1.3 collective-permute-start.2
  12.7 0.0 copy-start.1
  12.7 1.9 fusion.25
  14.6 7.8 %collective-permute-done.2 = bf16[2,128,256]{2,1,0:T(8,128)(2,1)S(1)} collective-permute-done((bf16[2,128,256]{2,1,0:T(8,128)(2,1)}, bf16[2,128,256]{2,1,0:T(8,128)(2,1)S(1)}, u32[]{:S(2)}, u32[]{:S(2)}) %collective-permute-start.2) | collective-permute-done | bytes 131104 | tf_op jit(solution)/shard_map/ppermute | solution.py:12
  22.4 1.7 fusion.29
  24.1 1.7 fusion.33
  25.8 0.0 copy-done.1
  25.9 0.0 copy-start
  25.9 0.6 fusion.3
  26.5 0.3 copy-done
  26.8 0.5 convolution_add_fusion.2
  27.2 0.5 convolution_add_fusion.1
  27.7 0.0 collective-permute-done.3
  27.7 0.5 fusion.11
  28.2 0.5 fusion.15
  28.7 0.0 copy-start.2
  28.7 0.0 copy-start.3
  28.7 0.0 copy-start.4
  28.7 0.6 fusion.4
  29.3 0.6 copy-done.2
  29.9 0.0 copy-done.3
  29.9 0.0 copy-done.4
  29.9 1.6 multiply_convert_fusion
  31.5 1.3 collective-permute-start.1
  32.8 6.0 %collective-permute-start = (bf16[2,128,2048]{2,1,0:T(8,128)(2,1)S(1)}, bf16[2,128,2048]{2,1,0:T(8,128)(2,1)S(1)}, u32[]{:S(2)}, u32[]{:S(2)}) collective-permute-start(bf16[2,128,2048]{2,1,0:T(8,128)(2,1)S(1)} %get-tuple-element.4), channel_id=1, source_target_pairs={{0,6},{1,7},{2,8},{3,9},{4,10},{5,11},{6,12},{7,13},{8,14},{9,15},... | collective-permute-start | bytes 3145736 | tf_op jit(solution)/shard_map/ppermute | solution.py:12
  38.9 0.5 convolution_bitcast_fusion.3
  39.4 0.5 convolution_bitcast_fusion.5
  39.9 0.5 convolution_bitcast_fusion.4
  40.4 0.4 maximum_bitcast_fusion.1
  40.8 33.5 %collective-permute-done = bf16[2,128,2048]{2,1,0:T(8,128)(2,1)S(1)} collective-permute-done((bf16[2,128,2048]{2,1,0:T(8,128)(2,1)S(1)}, bf16[2,128,2048]{2,1,0:T(8,128)(2,1)S(1)}, u32[]{:S(2)}, u32[]{:S(2)}) %collective-permute-start) | collective-permute-done | bytes 1048608 | tf_op jit(solution)/shard_map/ppermute | solution.py:12
  74.3 0.5 convolution_bitcast_fusion.6
  74.8 0.5 convolution_bitcast_fusion.8
  75.3 0.5 convolution_bitcast_fusion.7
  75.8 0.4 maximum_bitcast_fusion
  76.2 3.5 %collective-permute-done.1 = bf16[2,128,2048]{2,1,0:T(8,128)(2,1)S(1)} collective-permute-done((bf16[2,128,2048]{2,1,0:T(8,128)(2,1)S(1)}, bf16[2,128,2048]{2,1,0:T(8,128)(2,1)S(1)}, u32[]{:S(2)}, u32[]{:S(2)}) %collective-permute-start.1) | collective-permute-done | bytes 1048608 | tf_op jit(solution)/shard_map/ppermute | solution.py:12
  79.7 0.5 convolution_bitcast_fusion
  80.2 0.5 convolution_bitcast_fusion.2
  80.7 0.5 convolution_bitcast_fusion.1
  81.2 0.4 maximum_bitcast_fusion.2
  81.6 7.2 %pad_maximum_fusion = f32[3,3,2048,256]{3,2,1,0:T(8,128)} fusion(f32[1,3,2048,256]{3,2,1,0:T(8,128)S(1)} %maximum_bitcast_fusion.2, f32[1,3,2048,256]{3,2,1,0:T(8,128)S(1)} %maximum_bitcast_fusion.1, f32[1,3,2048,256]{3,2,1,0:T(8,128)S(1)} %maximum_bitcast_fusion), kind=kLoop, calls=%fused_computation | loop fusion | flops 9437184 | bytes 37748736 | tf_op jit(solution)/shard_map/stack | solution.py:56
  88.7 0.0 reduce-scatter.2.cloned.1.call-update
  88.8 1.7 fusion.27
  90.4 1.7 fusion.13
  92.1 1.7 fusion.31
  93.8 1.7 fusion.35
  95.5 1.7 fusion.9
  97.1 1.7 convolution_add_fusion.6
  98.8 1.9 convolution_add_fusion.5
  100.7 1.7 fusion.17
  102.4 2.6 fusion.10
  105.0 183.6 %reduce-scatter.2.cloned.1.call-done = f32[3,3,128,256]{3,2,1,0:T(8,128)} async-done(((f32[3,3,2048,256]{3,2,1,0:T(8,128)}), f32[3,3,128,256]{3,2,1,0:T(8,128)}) %reduce-scatter.2.cloned.1.call-update) | async-done | bytes 1179664 | tf_op jit(solution)/shard_map/reduce_scatter | solution.py:70
Async XLA Ops:
  7.2 281.4 %reduce-scatter.2.cloned.1.call-start = ((), (), s32[]{:S(2)}) async-start(), calls=%async_computation.1 | async-start | bytes 20054016 | tf_op jit(solution)/shard_map/reduce_scatter | solution.py:70
  7.2 20.5 %collective-permute-start.3 = (bf16[2,128,256]{2,1,0:T(8,128)(2,1)}, bf16[2,128,256]{2,1,0:T(8,128)(2,1)S(1)}, u32[]{:S(2)}, u32[]{:S(2)}) collective-permute-start(bf16[2,128,256]{2,1,0:T(8,128)(2,1)} %param.9), channel_id=1, source_target_pairs={{0,6},{1,7},{2,8},{3,9},{4,10},{5,11},{6,12},{7,13},{8,14},{9,15},... | collective-permute-start | bytes 393224 | tf_op jit(solution)/shard_map/ppermute | solution.py:12
  11.4 11.1 %collective-permute-start.2 = (bf16[2,128,256]{2,1,0:T(8,128)(2,1)}, bf16[2,128,256]{2,1,0:T(8,128)(2,1)S(1)}, u32[]{:S(2)}, u32[]{:S(2)}) collective-permute-start(bf16[2,128,256]{2,1,0:T(8,128)(2,1)} %param.9), channel_id=1, source_target_pairs={{6,0},{7,1},{8,2},{9,3},{10,4},{11,5},{12,6},{13,7},{14,8},{15,9},... | collective-permute-start | bytes 393224 | tf_op jit(solution)/shard_map/ppermute | solution.py:12
  12.7 13.2 %copy-start.1 = (bf16[3,3,2048,256]{3,2,1,0:T(8,128)(2,1)S(1)}, bf16[3,3,2048,256]{3,2,1,0:T(8,128)(2,1)}, u32[]{:S(2)}) copy-start(bf16[3,3,2048,256]{3,2,1,0:T(8,128)(2,1)} %param.8) | copy-start | bytes 28311556
  25.9 0.9 copy-start
  28.7 1.2 copy-start.2
  28.7 1.2 copy-start.3
  28.7 1.2 copy-start.4
  31.5 48.1 %collective-permute-start.1 = (bf16[2,128,2048]{2,1,0:T(8,128)(2,1)S(1)}, bf16[2,128,2048]{2,1,0:T(8,128)(2,1)S(1)}, u32[]{:S(2)}, u32[]{:S(2)}) collective-permute-start(bf16[2,128,2048]{2,1,0:T(8,128)(2,1)S(1)} %get-tuple-element.4), channel_id=1, source_target_pairs={{6,0},{7,1},{8,2},{9,3},{10,4},{11,5},{12,6},{13,7},{14,8},{15,9},... | collective-permute-start | bytes 3145736 | tf_op jit(solution)/shard_map/ppermute | solution.py:12
  32.8 41.5 %collective-permute-start = (bf16[2,128,2048]{2,1,0:T(8,128)(2,1)S(1)}, bf16[2,128,2048]{2,1,0:T(8,128)(2,1)S(1)}, u32[]{:S(2)}, u32[]{:S(2)}) collective-permute-start(bf16[2,128,2048]{2,1,0:T(8,128)(2,1)S(1)} %get-tuple-element.4), channel_id=1, source_target_pairs={{0,6},{1,7},{2,8},{3,9},{4,10},{5,11},{6,12},{7,13},{8,14},{9,15},... | collective-permute-start | bytes 3145736 | tf_op jit(solution)/shard_map/ppermute | solution.py:12
Sparse Core Ops, SparseCore 0:
  88.9 199.6 reduce-scatter.1
where the time goes:
time: 298 us; the launch traced here: 295 us
  waiting for transfers between devices  228 us (77%)
  matrix products  29.1 us (10%)
  between operations  14.3 us (5%)
  starting transfers between devices  12.8 us (4%)
  other arithmetic  10 us (3%)
    reduce_scatter x1, waiting for transfers between devices, per_device(): lax.psum_scatter(terms, 'rows', scatter_dimension=2, tiled=True)  184 us
    ppermute x4, waiting for transfers between devices, from_behind(): return lax.ppermute(array, axis, pairs)  44.8 us
    dot_general x9, matrix products, branch_forward(): jnp.einsum('hwc,ck->hwk', window, atrous_weight[row_tap, col_tap], prefer...  16.2 us
    ppermute x4, starting transfers between devices, from_behind(): return lax.ppermute(array, axis, pairs)  12.8 us
    dot_general x9, matrix products, spatial_act_grad(): jnp.einsum('hwk,ck->hwc', window, atrous_weight[row_tap, col_tap], prefer...  8.43 us
    another operation x4, other arithmetic, spatial_kernel_terms(): return jnp.stack(kernel_rows)  8.38 us
  transfers between devices with their start and end apart: 5, of which 4 were waited for; matrix products, arithmetic and copies ran while one was open for 9% of the time, Pallas kernels for 0%

commit v1 on v0

--- a/solution.py
+++ b/solution.py
@@ -1,9 +1,255 @@
+import functools
+
 import jax
 import jax.numpy as jnp
 from jax import lax
+from jax.experimental import pallas as pl
+from jax.experimental.pallas import tpu as pltpu
 from jax.sharding import PartitionSpec as P
 
 RATE = 12
+LANES = 128
+BF16 = jnp.bfloat16
+F32 = jnp.float32
+
+
+def col_shift(x, tap):
+    if tap == 1:
+        return x
+    rows, width, _ = x.shape
+    column = lax.broadcasted_iota(jnp.int32, x.shape[1:], 0)
+    if tap == 0:
+        amount, keep = RATE, column >= RATE
+    else:
+        amount, keep = width - RATE, column < width - RATE
+    return jnp.stack(
+        [jnp.where(keep, pltpu.roll(x[r], amount, 0), 0.0) for r in range(rows)]
+    )
+
+
+def fused_kernel(
+    n, rows, width, chans, outs,
+    feat_ref, scale_ref, shift_ref, w_hbm, cot_ref,
+    branch_ref, fgrad_ref, wgrad_ref,
+    w_ref, act_ref, send_ref, all_act, all_cot, cot_sh, part_ref, got_ref,
+    w_sem, act_send, act_recv, cot_send, cot_recv, part_send, part_recv,
+):
+    me = lax.axis_index("rows")
+    distance = RATE // rows
+    spots = rows * width
+    part_chans = chans // n
+
+    def shifted(x, tap):
+        return col_shift(x.reshape(rows, width, x.shape[1]), tap).reshape(x.shape)
+
+    def w_copy(tap):
+        return pltpu.make_async_copy(w_hbm.at[tap], w_ref.at[tap], w_sem.at[tap])
+
+    for tap in (0, 2, 1):
+        w_copy(tap).start()
+
+    barrier = pltpu.get_barrier_semaphore()
+
+    @pl.loop(1, n)
+    def _(k):
+        pl.semaphore_signal(
+            barrier, inc=1, device_id={"rows": lax.rem(me + k, n)},
+            device_id_type=pl.DeviceIdType.MESH,
+        )
+
+    def cot_copy(peer, source):
+        return pltpu.make_async_remote_copy(
+            src_ref=cot_ref, dst_ref=all_cot.at[source],
+            send_sem=cot_send.at[peer], recv_sem=cot_recv.at[source],
+            device_id={"rows": peer}, device_id_type=pl.DeviceIdType.MESH,
+        )
+
+    def act_copy(peer, source):
+        return pltpu.make_async_remote_copy(
+            src_ref=send_ref.at[peer], dst_ref=all_act.at[source],
+            send_sem=act_send.at[peer], recv_sem=act_recv.at[source],
+            device_id={"rows": peer}, device_id_type=pl.DeviceIdType.MESH,
+        )
+
+    def part_copy(tap):
+        return pltpu.make_async_remote_copy(
+            src_ref=part_ref.at[tap], dst_ref=got_ref.at[tap],
+            send_sem=part_send.at[tap], recv_sem=part_recv.at[tap],
+            device_id={"rows": jnp.clip(me - distance * (tap - 1), 0, n - 1)},
+            device_id_type=pl.DeviceIdType.MESH,
+        )
+
+    def inside(index):
+        return jnp.logical_and(index >= 0, index < n)
+
+    all_cot[me] = cot_ref[...]
+
+    @pl.loop(0, n)
+    def _(k):
+        cols = pl.ds(pl.multiple_of(k * part_chans, part_chans), part_chans)
+        pre = feat_ref[:, cols].astype(F32) * scale_ref[:, cols] + shift_ref[:, cols]
+        act = jnp.maximum(pre, 0.0).astype(BF16)
+        act_ref[:, cols] = act
+        send_ref[k] = act
+
+    all_act[me] = send_ref[me]
+
+    pl.semaphore_wait(barrier, n - 1)
+
+    @pl.loop(1, n)
+    def _(k):
+        cot_copy(lax.rem(me + k, n), me).start()
+
+    @pl.loop(1, n)
+    def _(k):
+        act_copy(lax.rem(me + k, n), me).start()
+
+    @pl.loop(0, 3)
+    def _(q):
+        tap = lax.rem(2 * q, 3)
+        w_copy(tap).wait()
+        total = jnp.zeros((spots, outs), F32)
+        for j in range(3):
+            total = total + shifted(
+                jnp.dot(act_ref[...], w_ref[tap, j], preferred_element_type=F32), j
+            )
+        part_ref[tap] = total
+
+        @pl.when(jnp.logical_and(tap != 1, inside(me - distance * (tap - 1))))
+        def _():
+            part_copy(tap).start()
+
+    @pl.loop(1, n)
+    def _(k):
+        source = lax.rem(me + n - k, n)
+        cot_copy(source, source).wait_recv()
+
+    for i in range(3):
+        source = me - distance * (i - 1)
+        block = all_cot[jnp.clip(source, 0, n - 1)].astype(F32)
+        block = jnp.where(inside(source), block, 0.0)
+        for j in range(3):
+            cot_sh[3 * i + j] = shifted(block, 2 - j).astype(BF16)
+
+    step = 256
+
+    @pl.loop(0, chans // step)
+    def _(b):
+        cols = pl.ds(pl.multiple_of(b * step, step), step)
+        total = jnp.zeros((spots, step), F32)
+        for i in range(3):
+            for j in range(3):
+                total = total + lax.dot_general(
+                    cot_sh[3 * i + j], w_ref[i, j, cols, :],
+                    (((1,), (1,)), ((), ())), preferred_element_type=F32,
+                )
+        scale = scale_ref[:, cols]
+        pre = feat_ref[:, cols].astype(F32) * scale + shift_ref[:, cols]
+        rounded = total.astype(BF16).astype(F32)
+        fgrad_ref[:, cols] = (scale * jnp.where(pre > 0, rounded, 0.0)).astype(BF16)
+
+    wgrad_ref[...] = jnp.zeros_like(wgrad_ref)
+
+    @pl.loop(0, n)
+    def _(k):
+        source = lax.rem(me + n - k, n)
+
+        @pl.when(k > 0)
+        def _():
+            act_copy(source, source).wait_recv()
+
+        block = all_act[source].astype(F32)
+        lhs = jnp.concatenate([shifted(block, j).astype(BF16) for j in range(3)], axis=1)
+        for i in range(3):
+            other = source - distance * (i - 1)
+
+            @pl.when(inside(other))
+            def _():
+                wgrad_ref[i] += lax.dot_general(
+                    lhs, all_cot[other], (((0,), (0,)), ((), ())),
+                    preferred_element_type=F32,
+                )
+
+    branch = part_ref[1]
+    branch_ref[...] = branch.astype(BF16)
+    for tap in (0, 2):
+
+        @pl.when(inside(me + distance * (tap - 1)))
+        def _():
+            part_copy(tap).wait_recv()
+
+        @pl.when(jnp.logical_not(inside(me + distance * (tap - 1))))
+        def _():
+            got_ref[tap] = jnp.zeros((spots, outs), F32)
+
+    branch_ref[...] = (part_ref[1] + got_ref[0] + got_ref[2]).astype(BF16)
+
+    for tap in (0, 2):
+
+        @pl.when(inside(me - distance * (tap - 1)))
+        def _():
+            part_copy(tap).wait_send()
+
+    @pl.loop(1, n)
+    def _(k):
+        peer = lax.rem(me + k, n)
+        cot_copy(peer, me).wait_send()
+        act_copy(peer, me).wait_send()
+
+
+def per_device_fused(features, bn_scale, bn_shift, atrous_weight, cotangent):
+    rows, width, chans = features.shape
+    outs = cotangent.shape[2]
+    n = lax.axis_size("rows")
+    spots = rows * width
+    part = chans // n
+    vmem = pl.BlockSpec(memory_space=pltpu.VMEM)
+    flops = 2 * 27 * spots * chans * outs
+    dma = pltpu.SemaphoreType.DMA
+    branch, fgrad, wgrad = pl.pallas_call(
+        functools.partial(fused_kernel, n, rows, width, chans, outs),
+        out_shape=(
+            jax.ShapeDtypeStruct((spots, outs), BF16),
+            jax.ShapeDtypeStruct((spots, chans), BF16),
+            jax.ShapeDtypeStruct((3, 3 * part, outs), F32),
+        ),
+        in_specs=[vmem, vmem, vmem, pl.BlockSpec(memory_space=pl.ANY), vmem],
+        out_specs=(vmem, vmem, vmem),
+        scratch_shapes=[
+            pltpu.VMEM(atrous_weight.shape, BF16),
+            pltpu.VMEM((spots, chans), BF16),
+            pltpu.VMEM((n, spots, part), BF16),
+            pltpu.VMEM((n, spots, part), BF16),
+            pltpu.VMEM((n, spots, outs), BF16),
+            pltpu.VMEM((9, spots, outs), BF16),
+            pltpu.VMEM((3, spots, outs), F32),
+            pltpu.VMEM((3, spots, outs), F32),
+            dma((3,)),
+            dma((n,)),
+            dma((n,)),
+            dma((n,)),
+            dma((n,)),
+            dma((3,)),
+            dma((3,)),
+        ],
+        compiler_params=pltpu.CompilerParams(
+            collective_id=0, has_side_effects=True, vmem_limit_bytes=50 * 2**20
+        ),
+        cost_estimate=pl.CostEstimate(
+            flops=flops, bytes_accessed=14 * 2**20, transcendentals=0
+        ),
+    )(
+        features.reshape(spots, chans),
+        bn_scale.reshape(1, chans),
+        bn_shift.reshape(1, chans),
+        atrous_weight,
+        cotangent.reshape(spots, outs),
+    )
+    return (
+        branch.reshape(rows, width, outs),
+        fgrad.reshape(rows, width, chans),
+        wgrad.reshape(3, 3, part, outs),
+    )
 
 
 def from_behind(array, axis, by):
@@ -56,7 +302,7 @@
     return jnp.stack(kernel_rows)
 
 
-def per_device(features, bn_scale, bn_shift, atrous_weight, cotangent):
+def per_device_plain(features, bn_scale, bn_shift, atrous_weight, cotangent):
     local_rows, width, chans = features.shape
     distance = RATE // local_rows
     pre_act = features.astype(jnp.float32) * bn_scale + bn_shift
@@ -74,6 +320,18 @@
     return (branch_out, feature_grad, weight_grad)
 
 
+def per_device(features, *others):
+    rows, width, chans = features.shape
+    fits = (
+        chans == LANES * lax.axis_size("rows")
+        and RATE % rows == 0
+        and width % 16 == 0
+        and width > RATE
+        and others[-1].shape[2] % LANES == 0
+    )
+    return (per_device_fused if fits else per_device_plain)(features, *others)
+
+
 def solution(mesh):
     return jax.shard_map(
         per_device,

time: 298 us -> 98.4 us (0.33)
  waiting for transfers between devices: 228 us -> 0 us
  Pallas kernels: 0 us -> 91.3 us
  matrix products: 29.1 us -> 0 us
  between operations: 14.3 us -> 0.65 us
  starting transfers between devices: 12.8 us -> 0 us
  other arithmetic: 10 us -> 0 us
  local copies, waits for them, and re-layouts: 0.86 us -> 6.15 us
    reduce_scatter x1 -> x0, waiting for transfers between devices: 184 us -> none  [per_device(): lax.psum_scatter(terms, 'rows', scatter_dimension=2, tiled=True)]
    pallas_call x0 -> x1, Pallas kernels: none -> 91.3 us  [per_device_fused(): pl.pallas_call(functools.partial(fused_kernel, n, rows, width, chans, out...]
    ppermute x4 -> x0, waiting for transfers between devices: 44.8 us -> none  [from_behind(): return lax.ppermute(array, axis, pairs)]
    dot_general x27 -> x0, matrix products: 29.1 us -> none  [the longest x9 16.2 us: branch_forward(): jnp.einsum('hwc,ck->hwk', window, atrous_weight[row_tap, col_tap], prefer...]
    ppermute x4 -> x0, starting transfers between devices: 12.8 us -> none  [from_behind(): return lax.ppermute(array, axis, pairs)]
    another operation x4 -> x0, other arithmetic: 8.38 us -> none  [spatial_kernel_terms(): return jnp.stack(kernel_rows)]
    unnamed x10 -> x11, local copies, waits for them, and re-layouts: 0.86 us -> 6.15 us
  transfers between devices with their start and end apart: 5 -> 0, of which waited for: 4 -> 0; matrix products, arithmetic and copies ran while one was open for 9% -> 0% of each run, Pallas kernels for 0% -> 0%
where the time goes in v1:
time: 98.4 us; the launch traced here: 98.2 us
  Pallas kernels  91.3 us (93%)
  local copies, waits for them, and re-layouts  6.15 us (6%)
    pallas_call x1, Pallas kernels, per_device_fused(): pl.pallas_call(functools.partial(fused_kernel, n, rows, width, chans, out...  91.3 us
    unnamed x11, local copies, waits for them, and re-layouts  6.15 us

profile of v1, /device:TPU:5, one launch (start us, length us, event | category | flops | bytes accessed | tf_op | source)
XLA Modules:
  0.0 98.2 jit_solution(2199812926979704473)
XLA Ops:
  0.6 0.0 copy-start
  0.6 1.2 %copy-done = bf16[2,128,2048]{2,1,0:T(8,128)(2,1)S(1)} copy-done((bf16[2,128,2048]{2,1,0:T(8,128)(2,1)S(1)}, bf16[2,128,2048]{2,1,0:T(8,128)(2,1)}, u32[]{:S(2)}) %copy-start) | copy-done | bytes 1048600
  1.9 0.0 copy-start.1
  1.9 0.9 copy-done.1
  2.8 0.0 copy-start.2
  2.8 0.7 copy-done.2
  3.5 0.0 copy-start.3
  3.5 0.7 copy-done.3
  4.2 91.3 %shard_map.76 = (bf16[256,256]{1,0:T(8,128)(2,1)S(1)}, bf16[256,2048]{1,0:T(8,128)(2,1)S(1)}, f32[3,384,256]{2,1,0:T(8,128)S(1)}) custom-call(bf16[256,2048]{1,0:T(8,128)(2,1)S(1)} %bitcast.10, f32[1,2048]{1,0:T(1,128)S(1)} %bitcast.12, f32[1,2048]{1,0:T(1,128)S(1)} %bitcast.13, bf16[3,3,2048,256]{3,2,1,0:T(8,128)(2,1)} %w_hbm.1, bf16[256,256]{1,0:T(8,128)(2,1)S(1)} %bitcast.11), custom_call_target="tpu_custom_call" | custom-call | flops 7247757312 | bytes 14680064 | tf_op jit(solution)/shard_map/pallas_call | solution.py:209
  95.5 0.7 copy.11
  96.2 1.0 copy.12
  97.1 1.0 %copy.13 = f32[3,3,128,256]{3,2,1,0:T(8,128)} copy(f32[3,3,128,256]{3,2,1,0:T(8,128)S(1)} %bitcast.7) | data formatting | bytes 2359296
Async XLA Ops:
  0.6 1.2 %copy-start = (bf16[2,128,2048]{2,1,0:T(8,128)(2,1)S(1)}, bf16[2,128,2048]{2,1,0:T(8,128)(2,1)}, u32[]{:S(2)}) copy-start(bf16[2,128,2048]{2,1,0:T(8,128)(2,1)} %param.5) | copy-start | bytes 3145732
  1.9 0.9 copy-start.1
  2.8 0.7 copy-start.2
  3.5 0.7 copy-start.3

commit v2 on v1

--- a/solution.py
+++ b/solution.py
@@ -29,15 +29,19 @@
 
 def fused_kernel(
     n, rows, width, chans, outs,
-    feat_ref, scale_ref, shift_ref, w_hbm, cot_ref,
+    feat_hbm, scale_ref, shift_ref, w_hbm, cot_hbm,
     branch_ref, fgrad_ref, wgrad_ref,
-    w_ref, act_ref, send_ref, all_act, all_cot, cot_sh, part_ref, got_ref,
-    w_sem, act_send, act_recv, cot_send, cot_recv, part_send, part_recv,
+    w_ref, feat_ref, act_ref, send_ref, all_act, all_cot, cot_sh, own_ref, part_ref, got_ref,
+    w_sem, feat_sem, act_send, act_recv, cot_send, cot_recv, part_send, part_recv,
 ):
     me = lax.axis_index("rows")
     distance = RATE // rows
     spots = rows * width
     part_chans = chans // n
+    slow = n // 4
+    mine, low = me // 4, lax.rem(me, 4)
+    other_mid = lax.rem(low + 2, 4)
+    other_core = low + 1 - 2 * lax.rem(low, 2)
 
     def shifted(x, tap):
         return col_shift(x.reshape(rows, width, x.shape[1]), tap).reshape(x.shape)
@@ -45,6 +49,10 @@
     def w_copy(tap):
         return pltpu.make_async_copy(w_hbm.at[tap], w_ref.at[tap], w_sem.at[tap])
 
+    feat_copy = pltpu.make_async_copy(feat_hbm, feat_ref, feat_sem.at[0])
+    own_cot_copy = pltpu.make_async_copy(cot_hbm, all_cot.at[me], feat_sem.at[1])
+    feat_copy.start()
+    own_cot_copy.start()
     for tap in (0, 2, 1):
         w_copy(tap).start()
 
@@ -57,12 +65,35 @@
             device_id_type=pl.DeviceIdType.MESH,
         )
 
-    def cot_copy(peer, source):
+    def cot_copy(way, source):
+        peer = (
+            jnp.minimum(me + 4, n - 4 + low),
+            jnp.maximum(me - 4, low),
+            4 * mine + other_mid,
+            4 * mine + other_core,
+        )[way]
         return pltpu.make_async_remote_copy(
-            src_ref=cot_ref, dst_ref=all_cot.at[source],
-            send_sem=cot_send.at[peer], recv_sem=cot_recv.at[source],
+            src_ref=all_cot.at[source], dst_ref=all_cot.at[source],
+            send_sem=cot_send.at[way, source], recv_sem=cot_recv.at[source],
             device_id={"rows": peer}, device_id_type=pl.DeviceIdType.MESH,
         )
+
+    def take_slow(hops):
+        for sign in (1, -1):
+            row = mine - sign * hops
+            source = 4 * row + low
+
+            @pl.when(jnp.logical_and(row >= 0, row < slow))
+            def _():
+                onward = 0 if sign == 1 else 1
+                cot_copy(onward, source).wait_recv()
+
+                @pl.when(jnp.logical_and(mine + sign >= 0, mine + sign < slow))
+                def _():
+                    cot_copy(onward, source).start()
+
+                cot_copy(2, source).start()
+                cot_copy(3, source).start()
 
     def act_copy(peer, source):
         return pltpu.make_async_remote_copy(
@@ -82,7 +113,7 @@
     def inside(index):
         return jnp.logical_and(index >= 0, index < n)
 
-    all_cot[me] = cot_ref[...]
+    feat_copy.wait()
 
     @pl.loop(0, n)
     def _(k):
@@ -96,9 +127,18 @@
 
     pl.semaphore_wait(barrier, n - 1)
 
-    @pl.loop(1, n)
-    def _(k):
-        cot_copy(lax.rem(me + k, n), me).start()
+    own_cot_copy.wait()
+
+    @pl.when(mine + 1 < slow)
+    def _():
+        cot_copy(0, me).start()
+
+    @pl.when(mine > 0)
+    def _():
+        cot_copy(1, me).start()
+
+    cot_copy(2, me).start()
+    cot_copy(3, me).start()
 
     @pl.loop(1, n)
     def _(k):
@@ -107,22 +147,33 @@
     @pl.loop(0, 3)
     def _(q):
         tap = lax.rem(2 * q, 3)
+        take_slow(q + 1)
         w_copy(tap).wait()
         total = jnp.zeros((spots, outs), F32)
         for j in range(3):
             total = total + shifted(
                 jnp.dot(act_ref[...], w_ref[tap, j], preferred_element_type=F32), j
             )
-        part_ref[tap] = total
+        part_ref[tap] = total.astype(BF16)
+
+        @pl.when(tap == 1)
+        def _():
+            own_ref[...] = total
 
         @pl.when(jnp.logical_and(tap != 1, inside(me - distance * (tap - 1))))
         def _():
             part_copy(tap).start()
 
-    @pl.loop(1, n)
-    def _(k):
-        source = lax.rem(me + n - k, n)
-        cot_copy(source, source).wait_recv()
+    @pl.loop(0, slow)
+    def _(k):
+        source = 4 * k + other_mid
+        cot_copy(2, source).wait_recv()
+        cot_copy(3, source).start()
+
+    @pl.loop(0, slow)
+    def _(k):
+        cot_copy(3, 4 * k + other_core).wait_recv()
+        cot_copy(3, 4 * k + lax.rem(other_core + 2, 4)).wait_recv()
 
     for i in range(3):
         source = me - distance * (i - 1)
@@ -170,8 +221,6 @@
                     preferred_element_type=F32,
                 )
 
-    branch = part_ref[1]
-    branch_ref[...] = branch.astype(BF16)
     for tap in (0, 2):
 
         @pl.when(inside(me + distance * (tap - 1)))
@@ -180,9 +229,9 @@
 
         @pl.when(jnp.logical_not(inside(me + distance * (tap - 1))))
         def _():
-            got_ref[tap] = jnp.zeros((spots, outs), F32)
-
-    branch_ref[...] = (part_ref[1] + got_ref[0] + got_ref[2]).astype(BF16)
+            got_ref[tap] = jnp.zeros((spots, outs), BF16)
+
+    branch_ref[...] = (own_ref[...] + got_ref[0].astype(F32) + got_ref[2].astype(F32)).astype(BF16)
 
     for tap in (0, 2):
 
@@ -193,8 +242,23 @@
     @pl.loop(1, n)
     def _(k):
         peer = lax.rem(me + k, n)
-        cot_copy(peer, me).wait_send()
         act_copy(peer, me).wait_send()
+
+    @pl.loop(0, slow)
+    def _(k):
+        source = 4 * k + low
+
+        @pl.when(jnp.logical_and(k <= mine, mine + 1 < slow))
+        def _():
+            cot_copy(0, source).wait_send()
+
+        @pl.when(jnp.logical_and(k >= mine, mine > 0))
+        def _():
+            cot_copy(1, source).wait_send()
+
+        cot_copy(2, source).wait_send()
+        cot_copy(3, source).wait_send()
+        cot_copy(3, 4 * k + other_mid).wait_send()
 
 
 def per_device_fused(features, bn_scale, bn_shift, atrous_weight, cotangent):
@@ -204,6 +268,7 @@
     spots = rows * width
     part = chans // n
     vmem = pl.BlockSpec(memory_space=pltpu.VMEM)
+    anywhere = pl.BlockSpec(memory_space=pl.ANY)
     flops = 2 * 27 * spots * chans * outs
     dma = pltpu.SemaphoreType.DMA
     branch, fgrad, wgrad = pl.pallas_call(
@@ -213,21 +278,24 @@
             jax.ShapeDtypeStruct((spots, chans), BF16),
             jax.ShapeDtypeStruct((3, 3 * part, outs), F32),
         ),
-        in_specs=[vmem, vmem, vmem, pl.BlockSpec(memory_space=pl.ANY), vmem],
+        in_specs=[anywhere, vmem, vmem, anywhere, anywhere],
         out_specs=(vmem, vmem, vmem),
         scratch_shapes=[
             pltpu.VMEM(atrous_weight.shape, BF16),
+            pltpu.VMEM((spots, chans), BF16),
             pltpu.VMEM((spots, chans), BF16),
             pltpu.VMEM((n, spots, part), BF16),
             pltpu.VMEM((n, spots, part), BF16),
             pltpu.VMEM((n, spots, outs), BF16),
             pltpu.VMEM((9, spots, outs), BF16),
-            pltpu.VMEM((3, spots, outs), F32),
-            pltpu.VMEM((3, spots, outs), F32),
+            pltpu.VMEM((spots, outs), F32),
+            pltpu.VMEM((3, spots, outs), BF16),
+            pltpu.VMEM((3, spots, outs), BF16),
             dma((3,)),
+            dma((2,)),
             dma((n,)),
             dma((n,)),
-            dma((n,)),
+            dma((4, n)),
             dma((n,)),
             dma((3,)),
             dma((3,)),
@@ -323,7 +391,8 @@
 def per_device(features, *others):
     rows, width, chans = features.shape
     fits = (
-        chans == LANES * lax.axis_size("rows")
+        lax.axis_size("rows") == 16
+        and chans == 16 * LANES
         and RATE % rows == 0
         and width % 16 == 0
         and width > RATE

time: 98.4 us -> 71.1 us (0.72)
  Pallas kernels: 91.3 us -> 64 us
    pallas_call x1, Pallas kernels: 91.3 us -> 64 us  [per_device_fused(): pl.pallas_call(functools.partial(fused_kernel, n, rows, width, chans, out...]
where the time goes in v2:
time: 71.1 us; the launch traced here: 70.8 us
  Pallas kernels  64 us (90%)
  local copies, waits for them, and re-layouts  6.15 us (9%)
    pallas_call x1, Pallas kernels, per_device_fused(): pl.pallas_call(functools.partial(fused_kernel, n, rows, width, chans, out...  64 us
    unnamed x11, local copies, waits for them, and re-layouts  6.15 us

profile of v2, /device:TPU:5, one launch (start us, length us, event | category | flops | bytes accessed | tf_op | source)
XLA Modules:
  0.0 70.8 jit_solution(10996507786515766498)
XLA Ops:
  0.6 0.0 copy-start
  0.6 1.2 %copy-done = bf16[2,128,2048]{2,1,0:T(8,128)(2,1)S(1)} copy-done((bf16[2,128,2048]{2,1,0:T(8,128)(2,1)S(1)}, bf16[2,128,2048]{2,1,0:T(8,128)(2,1)}, u32[]{:S(2)}) %copy-start) | copy-done | bytes 1048600
  1.9 0.0 copy-start.1
  1.9 0.9 %copy-done.1 = bf16[2,128,256]{2,1,0:T(8,128)(2,1)S(1)} copy-done((bf16[2,128,256]{2,1,0:T(8,128)(2,1)S(1)}, bf16[2,128,256]{2,1,0:T(8,128)(2,1)}, u32[]{:S(2)}) %copy-start.1) | copy-done | bytes 131096
  2.8 0.0 copy-start.2
  2.8 0.7 copy-done.2
  3.5 0.0 copy-start.3
  3.5 0.7 copy-done.3
  4.2 64.0 %shard_map.76 = (bf16[256,256]{1,0:T(8,128)(2,1)S(1)}, bf16[256,2048]{1,0:T(8,128)(2,1)S(1)}, f32[3,384,256]{2,1,0:T(8,128)S(1)}) custom-call(bf16[256,2048]{1,0:T(8,128)(2,1)S(1)} %bitcast.10, f32[1,2048]{1,0:T(1,128)S(1)} %bitcast.12, f32[1,2048]{1,0:T(1,128)S(1)} %bitcast.13, bf16[3,3,2048,256]{3,2,1,0:T(8,128)(2,1)} %w_hbm.1, bf16[256,256]{1,0:T(8,128)(2,1)S(1)} %bitcast.11), custom_call_target="tpu_custom_call" | custom-call | flops 7247757312 | bytes 14680064 | tf_op jit(solution)/shard_map/pallas_call | solution.py:274
  68.2 0.7 copy.11
  68.8 1.0 %copy.12 = bf16[2,128,2048]{2,1,0:T(8,128)(2,1)} copy(bf16[2,128,2048]{2,1,0:T(8,128)(2,1)S(1)} %bitcast.8) | data formatting | bytes 2097152
  69.8 1.0 %copy.13 = f32[3,3,128,256]{3,2,1,0:T(8,128)} copy(f32[3,3,128,256]{3,2,1,0:T(8,128)S(1)} %bitcast.7) | data formatting | bytes 2359296
Async XLA Ops:
  0.6 1.2 %copy-start = (bf16[2,128,2048]{2,1,0:T(8,128)(2,1)S(1)}, bf16[2,128,2048]{2,1,0:T(8,128)(2,1)}, u32[]{:S(2)}) copy-start(bf16[2,128,2048]{2,1,0:T(8,128)(2,1)} %param.5) | copy-start | bytes 3145732
  1.9 0.9 %copy-start.1 = (bf16[2,128,256]{2,1,0:T(8,128)(2,1)S(1)}, bf16[2,128,256]{2,1,0:T(8,128)(2,1)}, u32[]{:S(2)}) copy-start(bf16[2,128,256]{2,1,0:T(8,128)(2,1)} %param.9) | copy-start | bytes 393220
  2.8 0.7 copy-start.2
  3.5 0.7 copy-start.3

commit v3 on v2

--- a/solution.py
+++ b/solution.py
@@ -140,14 +140,18 @@
     cot_copy(2, me).start()
     cot_copy(3, me).start()
 
-    @pl.loop(1, n)
-    def _(k):
-        act_copy(lax.rem(me + k, n), me).start()
+    def send_acts(first, count):
+        @pl.loop(0, count)
+        def _(t):
+            act_copy(lax.rem(me + first + t, n), me).start()
+
+    send_acts(1, 1)
 
     @pl.loop(0, 3)
     def _(q):
         tap = lax.rem(2 * q, 3)
         take_slow(q + 1)
+        send_acts(2 + 1 * q, 1)
         w_copy(tap).wait()
         total = jnp.zeros((spots, outs), F32)
         for j in range(3):
@@ -170,10 +174,14 @@
         cot_copy(2, source).wait_recv()
         cot_copy(3, source).start()
 
+    send_acts(5, 4)
+
     @pl.loop(0, slow)
     def _(k):
         cot_copy(3, 4 * k + other_core).wait_recv()
         cot_copy(3, 4 * k + lax.rem(other_core + 2, 4)).wait_recv()
+
+    send_acts(9, 7)
 
     for i in range(3):
         source = me - distance * (i - 1)

time: 71.1 us -> 54.9 us (0.77); the launches traced: 70.8 us -> 53.8 us
  Pallas kernels: 64 us -> 47 us
    pallas_call x1, Pallas kernels: 64 us -> 47 us  [per_device_fused(): pl.pallas_call(functools.partial(fused_kernel, n, rows, width, chans, out...]
where the time goes in v3:
time: 54.9 us; the launch traced here: 53.8 us
  Pallas kernels  47 us (86%)
  local copies, waits for them, and re-layouts  6.15 us (11%)
  between operations  0.65 us (1%)
    pallas_call x1, Pallas kernels, per_device_fused(): pl.pallas_call(functools.partial(fused_kernel, n, rows, width, chans, out...  47 us
    unnamed x11, local copies, waits for them, and re-layouts  6.15 us

profile of v3, /device:TPU:5, one launch (start us, length us, event | category | flops | bytes accessed | tf_op | source)
XLA Modules:
  0.0 53.8 jit_solution(1771738302015277105)
XLA Ops:
  0.6 0.0 copy-start
  0.6 1.2 %copy-done = bf16[2,128,2048]{2,1,0:T(8,128)(2,1)S(1)} copy-done((bf16[2,128,2048]{2,1,0:T(8,128)(2,1)S(1)}, bf16[2,128,2048]{2,1,0:T(8,128)(2,1)}, u32[]{:S(2)}) %copy-start) | copy-done | bytes 1048600
  1.9 0.0 copy-start.1
  1.9 0.9 %copy-done.1 = bf16[2,128,256]{2,1,0:T(8,128)(2,1)S(1)} copy-done((bf16[2,128,256]{2,1,0:T(8,128)(2,1)S(1)}, bf16[2,128,256]{2,1,0:T(8,128)(2,1)}, u32[]{:S(2)}) %copy-start.1) | copy-done | bytes 131096
  2.8 0.0 copy-start.2
  2.8 0.7 %copy-done.2 = f32[2048]{0:T(1024)S(1)} copy-done((f32[2048]{0:T(1024)S(1)}, f32[2048]{0:T(1024)}, u32[]{:S(2)}) %copy-start.2) | copy-done | bytes 8216
  3.5 0.0 copy-start.3
  3.5 0.7 %copy-done.3 = f32[2048]{0:T(1024)S(1)} copy-done((f32[2048]{0:T(1024)S(1)}, f32[2048]{0:T(1024)}, u32[]{:S(2)}) %copy-start.3) | copy-done | bytes 8216
  4.2 47.0 %shard_map.76 = (bf16[256,256]{1,0:T(8,128)(2,1)S(1)}, bf16[256,2048]{1,0:T(8,128)(2,1)S(1)}, f32[3,384,256]{2,1,0:T(8,128)S(1)}) custom-call(bf16[256,2048]{1,0:T(8,128)(2,1)S(1)} %bitcast.10, f32[1,2048]{1,0:T(1,128)S(1)} %bitcast.12, f32[1,2048]{1,0:T(1,128)S(1)} %bitcast.13, bf16[3,3,2048,256]{3,2,1,0:T(8,128)(2,1)} %w_hbm.1, bf16[256,256]{1,0:T(8,128)(2,1)S(1)} %bitcast.11), custom_call_target="tpu_custom_call" | custom-call | flops 7247757312 | bytes 14680064 | tf_op jit(solution)/shard_map/pallas_call | solution.py:282
  51.2 0.7 %copy.11 = bf16[2,128,256]{2,1,0:T(8,128)(2,1)} copy(bf16[2,128,256]{2,1,0:T(8,128)(2,1)S(1)} %bitcast.9) | data formatting | bytes 262144
  51.8 1.0 %copy.12 = bf16[2,128,2048]{2,1,0:T(8,128)(2,1)} copy(bf16[2,128,2048]{2,1,0:T(8,128)(2,1)S(1)} %bitcast.8) | data formatting | bytes 2097152
  52.8 1.0 %copy.13 = f32[3,3,128,256]{3,2,1,0:T(8,128)} copy(f32[3,3,128,256]{3,2,1,0:T(8,128)S(1)} %bitcast.7) | data formatting | bytes 2359296
Async XLA Ops:
  0.6 1.2 %copy-start = (bf16[2,128,2048]{2,1,0:T(8,128)(2,1)S(1)}, bf16[2,128,2048]{2,1,0:T(8,128)(2,1)}, u32[]{:S(2)}) copy-start(bf16[2,128,2048]{2,1,0:T(8,128)(2,1)} %param.5) | copy-start | bytes 3145732
  1.9 0.9 %copy-start.1 = (bf16[2,128,256]{2,1,0:T(8,128)(2,1)S(1)}, bf16[2,128,256]{2,1,0:T(8,128)(2,1)}, u32[]{:S(2)}) copy-start(bf16[2,128,256]{2,1,0:T(8,128)(2,1)} %param.9) | copy-start | bytes 393220
  2.8 0.7 %copy-start.2 = (f32[2048]{0:T(1024)S(1)}, f32[2048]{0:T(1024)}, u32[]{:S(2)}) copy-start(f32[2048]{0:T(1024)} %param.6) | copy-start | bytes 24580
  3.5 0.7 %copy-start.3 = (f32[2048]{0:T(1024)S(1)}, f32[2048]{0:T(1024)}, u32[]{:S(2)}) copy-start(f32[2048]{0:T(1024)} %param.7) | copy-start | bytes 24580

commit v4 on v3

--- a/solution.py
+++ b/solution.py
@@ -174,14 +174,14 @@
         cot_copy(2, source).wait_recv()
         cot_copy(3, source).start()
 
-    send_acts(5, 4)
+    send_acts(5, 6)
 
     @pl.loop(0, slow)
     def _(k):
         cot_copy(3, 4 * k + other_core).wait_recv()
         cot_copy(3, 4 * k + lax.rem(other_core + 2, 4)).wait_recv()
 
-    send_acts(9, 7)
+    send_acts(11, 5)
 
     for i in range(3):
         source = me - distance * (i - 1)

time: 54.9 us -> 53.9 us (0.982)
  the two profiles are of different devices: /device:TPU:5 before, /device:TPU:29 now
where the time goes in v4:
time: 53.9 us; the launch traced here: 53.6 us
  Pallas kernels  46.8 us (87%)
  local copies, waits for them, and re-layouts  6.15 us (11%)
  between operations  0.65 us (1%)
    pallas_call x1, Pallas kernels, per_device_fused(): pl.pallas_call(functools.partial(fused_kernel, n, rows, width, chans, out...  46.8 us
    unnamed x11, local copies, waits for them, and re-layouts  6.15 us

profile of v4, /device:TPU:29, one launch (start us, length us, event | category | flops | bytes accessed | tf_op | source)
XLA Modules:
  0.0 53.6 jit_solution(6307147244057077079)
XLA Ops:
  0.6 0.0 copy-start
  0.6 1.2 %copy-done = bf16[2,128,2048]{2,1,0:T(8,128)(2,1)S(1)} copy-done((bf16[2,128,2048]{2,1,0:T(8,128)(2,1)S(1)}, bf16[2,128,2048]{2,1,0:T(8,128)(2,1)}, u32[]{:S(2)}) %copy-start) | copy-done | bytes 1048600
  1.9 0.0 copy-start.1
  1.9 0.9 %copy-done.1 = bf16[2,128,256]{2,1,0:T(8,128)(2,1)S(1)} copy-done((bf16[2,128,256]{2,1,0:T(8,128)(2,1)S(1)}, bf16[2,128,256]{2,1,0:T(8,128)(2,1)}, u32[]{:S(2)}) %copy-start.1) | copy-done | bytes 131096
  2.8 0.0 copy-start.2
  2.8 0.7 %copy-done.2 = f32[2048]{0:T(1024)S(1)} copy-done((f32[2048]{0:T(1024)S(1)}, f32[2048]{0:T(1024)}, u32[]{:S(2)}) %copy-start.2) | copy-done | bytes 8216
  3.5 0.0 copy-start.3
  3.5 0.7 %copy-done.3 = f32[2048]{0:T(1024)S(1)} copy-done((f32[2048]{0:T(1024)S(1)}, f32[2048]{0:T(1024)}, u32[]{:S(2)}) %copy-start.3) | copy-done | bytes 8216
  4.2 46.8 %shard_map.76 = (bf16[256,256]{1,0:T(8,128)(2,1)S(1)}, bf16[256,2048]{1,0:T(8,128)(2,1)S(1)}, f32[3,384,256]{2,1,0:T(8,128)S(1)}) custom-call(bf16[256,2048]{1,0:T(8,128)(2,1)S(1)} %bitcast.10, f32[1,2048]{1,0:T(1,128)S(1)} %bitcast.12, f32[1,2048]{1,0:T(1,128)S(1)} %bitcast.13, bf16[3,3,2048,256]{3,2,1,0:T(8,128)(2,1)} %w_hbm.1, bf16[256,256]{1,0:T(8,128)(2,1)S(1)} %bitcast.11), custom_call_target="tpu_custom_call" | custom-call | flops 7247757312 | bytes 14680064 | tf_op jit(solution)/shard_map/pallas_call | solution.py:282
  51.0 0.7 %copy.11 = bf16[2,128,256]{2,1,0:T(8,128)(2,1)} copy(bf16[2,128,256]{2,1,0:T(8,128)(2,1)S(1)} %bitcast.9) | data formatting | bytes 262144
  51.6 1.0 %copy.12 = bf16[2,128,2048]{2,1,0:T(8,128)(2,1)} copy(bf16[2,128,2048]{2,1,0:T(8,128)(2,1)S(1)} %bitcast.8) | data formatting | bytes 2097152
  52.6 1.0 %copy.13 = f32[3,3,128,256]{3,2,1,0:T(8,128)} copy(f32[3,3,128,256]{3,2,1,0:T(8,128)S(1)} %bitcast.7) | data formatting | bytes 2359296
Async XLA Ops:
  0.6 1.2 %copy-start = (bf16[2,128,2048]{2,1,0:T(8,128)(2,1)S(1)}, bf16[2,128,2048]{2,1,0:T(8,128)(2,1)}, u32[]{:S(2)}) copy-start(bf16[2,128,2048]{2,1,0:T(8,128)(2,1)} %param.5) | copy-start | bytes 3145732
  1.9 0.9 %copy-start.1 = (bf16[2,128,256]{2,1,0:T(8,128)(2,1)S(1)}, bf16[2,128,256]{2,1,0:T(8,128)(2,1)}, u32[]{:S(2)}) copy-start(bf16[2,128,256]{2,1,0:T(8,128)(2,1)} %param.9) | copy-start | bytes 393220
  2.8 0.7 %copy-start.2 = (f32[2048]{0:T(1024)S(1)}, f32[2048]{0:T(1024)}, u32[]{:S(2)}) copy-start(f32[2048]{0:T(1024)} %param.6) | copy-start | bytes 24580
  3.5 0.7 %copy-start.3 = (f32[2048]{0:T(1024)S(1)}, f32[2048]{0:T(1024)}, u32[]{:S(2)}) copy-start(f32[2048]{0:T(1024)} %param.7) | copy-start | bytes 24580
